TPU v7x, 32 devices: a whole 2x2x4 slice. The times are simulated.
32 devices in a mesh: row: 8 (over y, x, core), col: 4 (over z).
Axes of the slice: x: 2, y: 2, z: 4, core: 2. Of those that a mesh axis runs over, the one named last changes fastest.
Arguments:
- embeddings: float32 [4096, 256], P(('col', 'row')), may hold values from -6 to 6
- levels: int32 [4096], P('row'), may hold values from 0 to 7
Outputs:
- responsibility: float32 [4096, 4096], P('row', 'col')
- availability: float32 [4096, 4096], P('row', 'col')
All inputs are finite; a program needn't handle non-finite values.
Results may differ from a plain program's by a relative error of at most 0.0003.
Values sent between devices are 32-bit elements; how exact they have to be, the bound alone decides.
A program may use at most 64 MiB of HBM per device.

v0:
```python
import jax
import jax.numpy as jnp
from jax import lax
from jax.sharding import PartitionSpec as P

ITERS = 2


lowest_value = -1e30


def combined_all(part, axis, combine):
    gathered = jax.tree.map(lambda a: lax.all_gather(a, axis), part)

    def take(source):
        return jax.tree.map(lambda a: lax.dynamic_index_in_dim(a, source, 0, False), gathered)

    return lax.fori_loop(
        1, lax.axis_size(axis), lambda source, state: combine(state, take(source)), take(0)
    )


def normalize(vectors):
    return vectors * lax.rsqrt(jnp.sum(vectors * vectors, axis=1, keepdims=True) + 1e-06)


def top_two(values):
    best_value = jnp.max(values, axis=1, keepdims=True)
    tie_count = jnp.sum(jnp.where(values == best_value, 1, 0), axis=1, keepdims=True)
    remainder = jnp.max(jnp.where(values < best_value, values, lowest_value), axis=1, keepdims=True)
    return (best_value, jnp.where(tie_count > 1, best_value, remainder))


def combine_pairs(earlier_pair, later_pair):
    best_value = jnp.maximum(earlier_pair[0], later_pair[0])
    second_value = jnp.maximum(
        jnp.minimum(earlier_pair[0], later_pair[0]), jnp.maximum(earlier_pair[1], later_pair[1])
    )
    return (best_value, second_value)


def shards(embeddings, levels):
    row_count = levels.shape[0]
    n_row = lax.axis_size("row")
    n_col = lax.axis_size("col")
    row_idx = lax.axis_index("row")
    col_idx = lax.axis_index("col")
    span_rows = embeddings.shape[0]
    width = embeddings.shape[1]
    col_count = span_rows * n_row
    preference = 0.25 * levels.astype(jnp.float32) - 1.0
    every_point = lax.all_gather(embeddings, ("row", "col"), axis=0, tiled=True)
    ordered = (
        every_point.reshape(n_row, n_col, span_rows, width).transpose(1, 0, 2, 3).reshape(-1, width)
    )
    column_block = lax.dynamic_slice_in_dim(ordered, col_idx * col_count, col_count, 0)
    row_block = lax.dynamic_slice_in_dim(ordered, row_idx * row_count, row_count, 0)
    unit_rows = normalize(row_block)
    unit_cols = normalize(column_block)
    product = lax.dot_general(
        unit_rows,
        unit_cols,
        (((1,), (1,)), ((), ())),
        precision=lax.Precision.HIGHEST,
        preferred_element_type=jnp.float32,
    )
    global_rows = row_idx * row_count + jnp.arange(row_count, dtype=jnp.int32)
    global_cols = col_idx * col_count + jnp.arange(col_count, dtype=jnp.int32)
    diagonal_mask = global_rows[:, None] == global_cols[None, :]
    similar = jnp.where(diagonal_mask, preference[:, None], product)
    responsibility = jnp.zeros_like(similar)
    availability = jnp.zeros_like(similar)
    for iteration in range(ITERS):
        combined = availability + similar
        best_value, second_value = top_two(combined)
        best_value, second_value = combined_all((best_value, second_value), "col", combine_pairs)
        fresh = similar - jnp.where(combined >= best_value, second_value, best_value)
        responsibility = 0.5 * responsibility + 0.5 * fresh
        positive = jnp.sum(jnp.where(diagonal_mask, 0.0, jnp.maximum(responsibility, 0.0)), axis=0)
        diag_part = jnp.sum(jnp.where(diagonal_mask, responsibility, 0.0), axis=0)
        column_positive, self_resp = lax.psum((positive, diag_part), "row")
        renewed = jnp.where(
            diagonal_mask,
            column_positive[None, :],
            jnp.minimum(
                0.0,
                self_resp[None, :] + column_positive[None, :] - jnp.maximum(responsibility, 0.0),
            ),
        )
        availability = 0.5 * availability + 0.5 * renewed
    return (responsibility, availability)


def solution(mesh):
    placed = (P(("col", "row"), None), P("row"))
    return jax.shard_map(
        shards,
        mesh=mesh,
        in_specs=placed,
        out_specs=(P("row", "col"), P("row", "col")),
        check_vma=False,
    )
```

profile of v0, /device:TPU:0, one launch (start us, length us, event | category | flops | bytes accessed | tf_op | source)
XLA Modules:
  0.0 171.0 jit_solution(14361696423705120319)
XLA Ops:
  7.2 0.0 all-gather.10.cloned.1.call-start
  7.2 0.7 all-gather.10.cloned.1.call-update
  7.9 67.9 %all-gather.10.cloned.1.call-done = f32[4096,256]{1,0:T(8,128)} async-done(((f32[128,256]{1,0:T(8,128)}), f32[4096,256]{1,0:T(8,128)}) %all-gather.10.cloned.1.call-update) | async-done | bytes 4194320 | tf_op jit(solution)/shard_map/all_gather | solution.py:52
  75.8 0.0 copy-start.1
  75.8 2.6 %copy.5 = f32[4,8,128,256]{3,2,1,0:T(8,128)S(1)} copy(f32[4,8,128,256]{3,2,0,1:T(8,128)} %bitcast.53) | data formatting | bytes 8388608 | tf_op jit(solution)/shard_map/transpose | solution.py:54
  78.4 0.2 multiply_reduce_fusion.1
  78.6 0.2 multiply_reduce_fusion
  78.8 0.0 copy-done.1
  78.8 2.2 %fusion.19 = (f32[512]{0:T(512)S(1)}, f32[512,1024]{1,0:T(8,128)S(1)}) fusion(f32[4096,256]{1,0:T(8,128)S(1)} %bitcast.52, s32[]{:T(128)S(6)} %select_n.104, f32[1024]{0:T(1024)S(1)} %add_rsqrt_fusion, s32[]{:T(128)S(6)} %select_n.103, f32[512]{0:T(512)S(1)} %get-tuple-element.309, f32[512]{0:T(512)S(1)} %get-tuple-element.310, s32[1024]{0:T(1024)S(1)} %iota_add_fusion, ...), kind=kOutput, calls=%fused_computation.52 | convolution fusion | flops 1612578304 | bytes 3686408 | tf_op jit(solution)/shard_map/dot_general | solution.py:60
  81.0 0.4 select_reduce_fusion.1
  81.4 0.4 fusion.8
  81.7 11.9 %all-gather.5 = f32[4,1,512]{2,1,0:T(1,128)S(1)} all-gather(f32[1,1,512]{2,1,0:T(1,128)S(1)} %bitcast.70), channel_id=4, replica_groups=mesh['row'=8,'col'=4] {'col'}, dimensions={0}, use_global_device_ids=true | all-gather | bytes 10240 | tf_op jit(solution)/shard_map/all_gather | solution.py:13
  93.6 11.9 %all-gather.4 = f32[4,1,512]{2,1,0:T(1,128)S(1)} all-gather(f32[1,1,512]{2,1,0:T(1,128)S(1)} %bitcast.69), channel_id=2, replica_groups=mesh['row'=8,'col'=4] {'col'}, dimensions={0}, use_global_device_ids=true | all-gather | bytes 10240 | tf_op jit(solution)/shard_map/all_gather | solution.py:13
  105.5 0.1 while.34
  105.6 0.8 fusion.2
  106.4 12.0 %all-reduce.1 = (f32[1024]{0:T(1024)S(1)}, f32[1024]{0:T(1024)S(1)}) all-reduce(f32[1024]{0:T(1024)S(1)} %get-tuple-element.273, f32[1024]{0:T(1024)S(1)} %get-tuple-element.272), channel_id=1, replica_groups=mesh['row'=8,'col'=4] {'row'}, use_global_device_ids=true, to_apply=%region_10.11 | all-reduce | flops 2048 | bytes 16384 | tf_op jit(solution)/shard_map/psum | solution.py:81
  118.4 1.1 fusion.18
  119.6 0.0 copy-start
  119.6 0.4 select_reduce_fusion
  120.0 0.4 fusion.9
  120.4 0.5 copy-done
  120.9 11.9 %all-gather.7 = f32[4,1,512]{2,1,0:T(1,128)S(1)} all-gather(f32[1,1,512]{2,1,0:T(1,128)S(1)} %bitcast.71), channel_id=5, replica_groups=mesh['row'=8,'col'=4] {'col'}, dimensions={0}, use_global_device_ids=true | all-gather | bytes 10240 | tf_op jit(solution)/shard_map/all_gather | solution.py:13
  132.8 11.9 %all-gather.6 = f32[4,1,512]{2,1,0:T(1,128)S(1)} all-gather(f32[1,1,512]{2,1,0:T(1,128)S(1)} %bitcast.64), channel_id=3, replica_groups=mesh['row'=8,'col'=4] {'col'}, dimensions={0}, use_global_device_ids=true | all-gather | bytes 10240 | tf_op jit(solution)/shard_map/all_gather | solution.py:13
  144.6 0.1 while.35
  144.7 3.4 %fusion.4 = (f32[1024]{0:T(1024)S(1)}, f32[1024]{0:T(1024)S(1)}, f32[512,1024]{1,0:T(8,128)}) fusion(s32[1024]{0:T(1024)S(1)} %iota_add_fusion, s32[512]{0:T(512)S(1)} %iota_add_fusion.1, f32[512,1024]{1,0:T(8,128)S(1)} %get-tuple-element.308, f32[512]{0:T(512)S(1)} %bitcast.62, f32[512,1024]{1,0:T(8,128)} %copy-done, f32[512]{0:T(512)S(1)} %bitcast.63, ...), kind=kLoop, calls=%fused_computation.19 | loop fusion | flops 7862272 | bytes 6313984 | tf_op jit(solution)/shard_map/reduce_sum | solution.py:79
  148.1 12.0 %all-reduce = (f32[1024]{0:T(1024)S(1)}, f32[1024]{0:T(1024)S(1)}) all-reduce(f32[1024]{0:T(1024)S(1)} %get-tuple-element.275, f32[1024]{0:T(1024)S(1)} %get-tuple-element.274), channel_id=1, replica_groups=mesh['row'=8,'col'=4] {'row'}, use_global_device_ids=true, to_apply=%region_19.20 | all-reduce | flops 2048 | bytes 16384 | tf_op jit(solution)/shard_map/psum | solution.py:81
  160.2 4.0 %fusion.7 = f32[512,1024]{1,0:T(8,128)} fusion(f32[512,1024]{1,0:T(8,128)} %get-tuple-element.300, f32[512,1024]{1,0:T(8,128)S(1)} %get-tuple-element.308, f32[1024]{0:T(1024)S(1)} %add.160, f32[1024]{0:T(1024)S(1)} %get-tuple-element.297, f32[1024]{0:T(1024)S(1)} %add.157, f32[1024]{0:T(1024)S(1)} %get-tuple-element.299, f32[512]{0:T(512)S(1)} %bitcast.57, ...), kind=kLoop, calls=%fused_computation.22 | loop fusion | flops 8388608 | bytes 6318080 | tf_op jit(solution)/shard_map/add | solution.py:90
  (18 shorter events, 0.2 us)
Async XLA Ops:
  7.2 68.7 %all-gather.10.cloned.1.call-start = ((), (), s32[]{:S(2)}) async-start(), calls=%async_computation | async-start | bytes 4325376 | tf_op jit(solution)/shard_map/all_gather | solution.py:52
  75.8 3.0 %copy-start.1 = (s32[512]{0:T(512)S(1)}, s32[512]{0:T(512)}, u32[]{:S(2)}) copy-start(s32[512]{0:T(512)} %param.7) | copy-start | bytes 6148
  119.6 1.3 copy-start
Sparse Core Ops, SparseCore 0:
  11.0 64.7 all-gather.9
where the time goes:
time: 171 us
  blocking collectives  71.5 us (42%)
  waiting for transfers between devices  68.6 us (40%)
  between operations  14.2 us (8%)
  other arithmetic  11.4 us (7%)
  local copies, waits for them, and re-layouts  3.1 us (2%)
  matrix products  2.17 us (1%)
    all_gather x1, waiting for transfers between devices, shards(): every_point = lax.all_gather(embeddings, ('row', 'col'), axis=0, tiled=True)  67.9 us
    all_gather x4, blocking collectives, combined_all(): gathered = jax.tree.map(lambda a: lax.all_gather(a, axis), part)  47.5 us
    psum x2, blocking collectives, shards(): column_positive, self_resp = lax.psum((positive, diag_part), 'row')  24.1 us
    reduce_sum x2, other arithmetic, shards(): jnp.sum(jnp.where(diagonal_mask, 0.0, jnp.maximum(responsibility, 0.0)),...  4.17 us
    add x1, other arithmetic, shards(): availability = 0.5 * availability + 0.5 * renewed  3.99 us
  transfers between devices with their start and end apart: 1, of which 1 were waited for; matrix products, arithmetic and copies ran while one was open for 0% of the time, Pallas kernels for 0%

commit v1 on v0

v1 whole, which is shorter than its diff:
```python
import functools

import jax
import jax.numpy as jnp
from jax import lax
from jax.experimental import pallas as pl
from jax.experimental.pallas import tpu as pltpu
from jax.sharding import PartitionSpec as P

ITERS = 2
LANES = 128
STEP = 32
LOWEST = -1e30
MESH = pl.DeviceIdType.MESH


def kernel(
    n_row, n_col, emb, levels, resp_out, avail_out,
    cols, zbuf, rows, cols_cat, rows_cat, sim, resp, avail, best, second, tops, sums,
    zs, zr, cs, cr, fs, rs, rr, ts, tr, us, ur, outs, local,
):
    span, width = emb.shape
    row_count, col_count = sim.shape
    groups, chunks = row_count // LANES, col_count // LANES
    per = n_row // n_col
    r, c = lax.axis_index("row"), lax.axis_index("col")
    sibling = r + 1 - 2 * lax.rem(r, 2)

    def at_row(o):
        return lax.rem(r + o, n_row)

    def at_col(o):
        return lax.rem(c + o, n_col)

    barrier = pltpu.get_barrier_semaphore()
    for o in range(1, n_row):
        pl.semaphore_signal(barrier, inc=1, device_id=(at_row(o), c), device_id_type=MESH)
    for o in range(1, n_col):
        pl.semaphore_signal(barrier, inc=1, device_id=(r, at_col(o)), device_id_type=MESH)

    def part(index):
        return pl.ds(pl.multiple_of(index * span, span), span)

    own = emb[...]
    cols[part(r), :] = own * lax.rsqrt(jnp.sum(own * own, axis=1, keepdims=True) + 1e-06)
    pl.semaphore_wait(barrier, n_row + n_col - 2)

    def col_copy(block, send, target):
        return pltpu.make_async_remote_copy(
            src_ref=cols.at[part(block), :], dst_ref=cols.at[part(block), :],
            send_sem=send, recv_sem=cr.at[block], device_id=(target, c), device_id_type=MESH,
        )

    def z_copy(o, slot):
        return pltpu.make_async_remote_copy(
            src_ref=cols.at[part(r), :], dst_ref=zbuf.at[slot],
            send_sem=zs.at[o], recv_sem=zr.at[slot], device_id=(r, at_col(o)), device_id_type=MESH,
        )

    def row_copy(o, slot, place, target):
        return pltpu.make_async_remote_copy(
            src_ref=zbuf.at[slot], dst_ref=rows.at[part(place), :],
            send_sem=rs.at[o], recv_sem=rr.at[place], device_id=(target, c), device_id_type=MESH,
        )

    half = n_row // 2
    for o in range(1, n_col):
        z_copy(o, c).start()
    for o in range(1, half):
        col_copy(r, cs.at[o], at_row(2 * o)).start()
    col_copy(r, cs.at[0], sibling).start()

    place = lax.rem(r, n_col)

    def target_of(o):
        slot = at_col(n_col - o)
        return slot, slot * per + r // n_col

    for o in range(1, half):
        source = at_row(n_row - 2 * o)
        col_copy(source, fs.at[o], sibling).wait_recv()
        col_copy(source, fs.at[o], sibling).start()
    for o in range(1, n_col):
        slot, target = target_of(o)
        z_copy(o, slot).wait_recv()

        @pl.when(target != r)
        def _():
            row_copy(o, slot, place, target).start()

        @pl.when(target == r)
        def _():
            pltpu.make_async_copy(zbuf.at[slot], rows.at[part(place), :], local).start()
            pltpu.make_async_copy(zbuf.at[slot], rows.at[part(place), :], local).wait()

    col_copy(sibling, cs.at[0], sibling).wait_recv()
    for o in range(1, half):
        col_copy(lax.rem(sibling + n_row - 2 * o, n_row), fs.at[o], sibling).wait_recv()

    def split(ref):
        value = ref[...]
        high = value.astype(jnp.bfloat16)
        return high, (value - high.astype(jnp.float32)).astype(jnp.bfloat16)

    high, low = split(cols)
    cols_cat[:, :width] = high
    cols_cat[:, width : 2 * width] = low
    cols_cat[:, 2 * width :] = high

    source_col = r // per
    first = lax.rem(r, per) * n_col

    @pl.when(source_col == c)
    def _():
        for q in range(n_col):
            rows[q * span : (q + 1) * span, :] = cols[part(first + q), :]

    @pl.when(source_col != c)
    def _():
        for q in range(n_col):

            @pl.when(first + q != r)
            def _():
                row_copy(0, c, q, sibling).wait_recv()

    high, low = split(rows)
    rows_cat[:, :width] = high
    rows_cat[:, width : 2 * width] = high
    rows_cat[:, 2 * width :] = low

    wide = 2 * LANES

    @pl.loop(0, col_count // wide)
    def _(k):
        lanes = pl.ds(pl.multiple_of(k * wide, wide), wide)
        sim[:, lanes] = lax.dot_general(
            rows_cat[...], cols_cat[lanes, :], (((1,), (1,)), ((), ())),
            preferred_element_type=jnp.float32,
        )

    offset = r * row_count - c * col_count
    on_diagonal = (offset >= 0) & (offset < col_count)
    eye = lax.broadcasted_iota(jnp.int32, (LANES, LANES), 0) == lax.broadcasted_iota(
        jnp.int32, (LANES, LANES), 1
    )
    slant = lax.broadcasted_iota(jnp.int32, (STEP, LANES), 1) - lax.broadcasted_iota(
        jnp.int32, (STEP, LANES), 0
    )

    def tile_of(g):
        return (
            pl.ds(g * LANES, LANES),
            pl.ds(pl.multiple_of(offset + g * LANES, LANES), LANES),
        )

    @pl.when(on_diagonal)
    def _():
        preference = 0.25 * levels[...].astype(jnp.float32) - 1.0
        for g in range(groups):
            tile = tile_of(g)
            sim[tile] = jnp.where(eye, preference[g : g + 1, :], sim[tile])

    def spread(value):
        return jnp.broadcast_to(value, (value.shape[0], LANES))

    def lanes_of(k):
        return pl.ds(k * LANES, LANES)

    def rows_at(i):
        return pl.ds(pl.multiple_of(i * STEP, STEP), STEP)

    def top_pass(entry):
        @pl.loop(0, row_count // STEP)
        def _(i):
            here = rows_at(i)
            one = entry(i, here, 0)
            two = jnp.full_like(one, LOWEST)
            for k in range(1, chunks):
                value = entry(i, here, k)
                two = jnp.maximum(two, jnp.minimum(one, value))
                one = jnp.maximum(one, value)
            top = jnp.max(one, axis=1, keepdims=True)
            count = jnp.sum(jnp.where(one == top, 1.0, 0.0), axis=1, keepdims=True)
            rest = jnp.max(
                jnp.maximum(jnp.where(one < top, one, LOWEST), two), axis=1, keepdims=True
            )
            best[here, :] = spread(top)
            second[here, :] = spread(jnp.where(count > 1.0, top, rest))

    def top_exchange(turn):
        for g in range(groups):
            for ref, base in ((best, 0), (second, groups)):
                tops[turn, c, base + g : base + g + 1, :] = jnp.sum(
                    jnp.where(eye, ref[g * LANES : (g + 1) * LANES, :], 0.0), axis=0, keepdims=True
                )

        def copy(o, slot):
            return pltpu.make_async_remote_copy(
                src_ref=tops.at[turn, c], dst_ref=tops.at[turn, slot],
                send_sem=ts.at[turn, o], recv_sem=tr.at[turn, slot],
                device_id=(r, at_col(o)), device_id_type=MESH,
            )

        for o in range(1, n_col):
            copy(o, c).start()
        for o in range(1, n_col):
            copy(o, at_col(n_col - o)).wait_recv()
        one, two = tops[turn, 0, :groups, :], tops[turn, 0, groups:, :]
        for q in range(1, n_col):
            other, another = tops[turn, q, :groups, :], tops[turn, q, groups:, :]
            two = jnp.maximum(jnp.minimum(one, other), jnp.maximum(two, another))
            one = jnp.maximum(one, other)
        for g in range(groups):
            for ref, value in ((best, one), (second, two)):
                ref[g * LANES : (g + 1) * LANES, :] = spread(
                    jnp.sum(jnp.where(eye, value[g : g + 1, :], 0.0), axis=1, keepdims=True)
                )
        return lambda: [copy(o, c).wait_send() for o in range(1, n_col)]

    def resp_pass(turn):
        for k in range(chunks):
            lanes = lanes_of(k)

            def body(i, total):
                here = rows_at(i)
                similar = sim[here, lanes]
                combined = similar if turn == 0 else avail[here, lanes] + similar
                fresh = similar - jnp.where(combined >= best[here, :], second[here, :], best[here, :])
                updated = 0.5 * fresh if turn == 0 else 0.5 * resp[here, lanes] + 0.5 * fresh
                resp[here, lanes] = updated
                positive = jnp.where(
                    slant == offset + i * STEP - k * LANES, 0.0, jnp.maximum(updated, 0.0)
                )
                return total + jnp.sum(positive.reshape(STEP // 8, 8, LANES), axis=0)

            total = lax.fori_loop(
                0, row_count // STEP, body, jnp.zeros((8, LANES), jnp.float32), unroll=2
            )
            sums[turn, r, k : k + 1, :] = jnp.sum(total, axis=0, keepdims=True)
        sums[turn, r, chunks:, :] = jnp.zeros((chunks, LANES), jnp.float32)

        @pl.when(on_diagonal)
        def _():
            for g in range(groups):
                sums[turn, r, pl.ds(chunks + offset // LANES + g, 1), :] = jnp.sum(
                    jnp.where(eye, resp[tile_of(g)], 0.0), axis=0, keepdims=True
                )

    def sum_copy(turn, o, slot):
        return pltpu.make_async_remote_copy(
            src_ref=sums.at[turn, r], dst_ref=sums.at[turn, slot],
            send_sem=us.at[turn, o], recv_sem=ur.at[turn, slot],
            device_id=(at_row(o), c), device_id_type=MESH,
        )

    def sum_exchange(turn):
        for o in range(1, n_row):
            sum_copy(turn, o, r).start()
        for o in range(1, n_row):
            sum_copy(turn, o, at_row(n_row - o)).wait_recv()
        total = sums[turn, 0]
        for q in range(1, n_row):
            total = total + sums[turn, q]
        positive = total[:chunks, :]
        return positive, total[chunks:, :] + positive

    def renewed(stats, i, here, k):
        positive, both = stats
        return jnp.where(
            slant == offset + i * STEP - k * LANES,
            positive[k : k + 1, :],
            jnp.minimum(0.0, both[k : k + 1, :] - jnp.maximum(resp[here, lanes_of(k)], 0.0)),
        )

    top_pass(lambda i, here, k: sim[here, lanes_of(k)])
    tops_sent = [top_exchange(0)]
    resp_pass(0)
    stats = sum_exchange(0)

    def second_entry(i, here, k):
        value = 0.5 * renewed(stats, i, here, k)
        avail[here, lanes_of(k)] = value
        return value + sim[here, lanes_of(k)]

    top_pass(second_entry)
    tops_sent.append(top_exchange(1))
    resp_pass(1)
    resp_copy = pltpu.make_async_copy(resp, resp_out, local)
    for o in range(1, n_row):
        sum_copy(1, o, r).start()
    resp_copy.start()
    for o in range(1, n_row):
        sum_copy(1, o, at_row(n_row - o)).wait_recv()
    total = sums[1, 0]
    for q in range(1, n_row):
        total = total + sums[1, q]
    positive = total[:chunks, :]
    last = (positive, total[chunks:, :] + positive)

    def out_copy(g):
        piece = pl.ds(g * LANES, LANES)
        return pltpu.make_async_copy(avail.at[piece, :], avail_out.at[piece, :], outs.at[g])

    for g in range(groups):

        @pl.loop(g * (LANES // STEP), (g + 1) * (LANES // STEP))
        def _(i):
            here = rows_at(i)
            for k in range(chunks):
                lanes = lanes_of(k)
                avail[here, lanes] = 0.5 * avail[here, lanes] + 0.5 * renewed(last, i, here, k)

        out_copy(g).start()

    for o in range(1, n_col):
        z_copy(o, c).wait_send()
        slot, target = target_of(o)

        @pl.when(target != r)
        def _():
            row_copy(o, slot, place, target).wait_send()

    for o in range(1, half):
        col_copy(r, cs.at[o], at_row(2 * o)).wait_send()
        col_copy(at_row(n_row - 2 * o), fs.at[o], sibling).wait_send()
    col_copy(r, cs.at[0], sibling).wait_send()
    for sent in tops_sent:
        sent()
    for turn in range(ITERS):
        for o in range(1, n_row):
            sum_copy(turn, o, r).wait_send()
    resp_copy.wait()
    for g in range(groups):
        out_copy(g).wait()


def shards(embeddings, levels):
    n_row, n_col = lax.axis_size("row"), lax.axis_size("col")
    span, width = embeddings.shape
    row_count = levels.shape[0]
    col_count = span * n_row
    groups, chunks = row_count // LANES, col_count // LANES
    full = jax.ShapeDtypeStruct((row_count, col_count), jnp.float32)
    dma = pltpu.SemaphoreType.DMA
    return pl.pallas_call(
        functools.partial(kernel, n_row, n_col),
        out_shape=(full, full),
        in_specs=[pl.BlockSpec(memory_space=pltpu.VMEM)] * 2,
        out_specs=[pl.BlockSpec(memory_space=pl.ANY)] * 2,
        scratch_shapes=[
            pltpu.VMEM((col_count, width), jnp.float32),
            pltpu.VMEM((n_col, span, width), jnp.float32),
            pltpu.VMEM((row_count, width), jnp.float32),
            pltpu.VMEM((col_count, 3 * width), jnp.bfloat16),
            pltpu.VMEM((row_count, 3 * width), jnp.bfloat16),
            pltpu.VMEM((row_count, col_count), jnp.float32),
            pltpu.VMEM((row_count, col_count), jnp.float32),
            pltpu.VMEM((row_count, col_count), jnp.float32),
            pltpu.VMEM((row_count, LANES), jnp.float32),
            pltpu.VMEM((row_count, LANES), jnp.float32),
            pltpu.VMEM((ITERS, n_col, 2 * groups, LANES), jnp.float32),
            pltpu.VMEM((ITERS, n_row, 2 * chunks, LANES), jnp.float32),
            dma((n_col,)), dma((n_col,)),
            dma((n_row,)), dma((n_row,)), dma((n_row,)),
            dma((n_col,)), dma((n_col,)),
            dma((ITERS, n_col)), dma((ITERS, n_col)),
            dma((ITERS, n_row)), dma((ITERS, n_row)),
            dma((groups,)), dma,
        ],
        compiler_params=pltpu.CompilerParams(
            collective_id=0, has_side_effects=True, vmem_limit_bytes=58 * 1024 * 1024
        ),
        cost_estimate=pl.CostEstimate(
            flops=6 * row_count * col_count * width,
            bytes_accessed=8 * row_count * col_count,
            transcendentals=0,
        ),
    )(embeddings, levels.reshape(groups, LANES))


def solution(mesh):
    return jax.shard_map(
        shards,
        mesh=mesh,
        in_specs=(P(("col", "row"), None), P("row")),
        out_specs=(P("row", "col"), P("row", "col")),
        check_vma=False,
    )
```

time: 171 us -> 57.6 us (0.34)
  blocking collectives: 71.5 us -> 0 us
  waiting for transfers between devices: 68.6 us -> 0 us
  Pallas kernels: 0 us -> 52.1 us
  between operations: 14.2 us -> 0.65 us
  other arithmetic: 11.4 us -> 0 us
  matrix products: 2.17 us -> 0 us
    all_gather x1 -> x0, waiting for transfers between devices: 67.9 us -> none  [shards(): every_point = lax.all_gather(embeddings, ('row', 'col'), axis=0, tiled=True)]
    pallas_call x0 -> x1, Pallas kernels: none -> 52.1 us  [shards(): pl.pallas_call(functools.partial(kernel, n_row, n_col), out_shape=(full,...]
    all_gather x4 -> x0, blocking collectives: 47.5 us -> none  [combined_all(): gathered = jax.tree.map(lambda a: lax.all_gather(a, axis), part)]
    psum x2 -> x0, blocking collectives: 24.1 us -> none  [shards(): column_positive, self_resp = lax.psum((positive, diag_part), 'row')]
    reduce_sum x6 -> x0, other arithmetic: 5.34 us -> none  [the longest x2 4.17 us: shards(): jnp.sum(jnp.where(diagonal_mask, 0.0, jnp.maximum(responsibility, 0.0)),...]
    unnamed x4, local copies, waits for them, and re-layouts: 0.54 us -> 4.63 us
    add x5 -> x0, other arithmetic: 4 us -> none  [the longest x1 3.99 us: shards(): availability = 0.5 * availability + 0.5 * renewed]
    transpose x1 -> x0, local copies, waits for them, and re-layouts: 2.56 us -> none  [shards(): every_point.reshape(n_row, n_col, span_rows, width).transpose(1, 0, 2, 3)]
  transfers between devices with their start and end apart: 1 -> 0, of which waited for: 1 -> 0; matrix products, arithmetic and copies ran while one was open for 0% -> 0% of each run, Pallas kernels for 0% -> 0%
where the time goes in v1:
time: 57.6 us; the launch traced here: 57.4 us
  Pallas kernels  52.1 us (90%)
  local copies, waits for them, and re-layouts  4.63 us (8%)
  between operations  0.65 us (1%)
    pallas_call x1, Pallas kernels, shards(): pl.pallas_call(functools.partial(kernel, n_row, n_col), out_shape=(full,...  52.1 us
    unnamed x4, local copies, waits for them, and re-layouts  4.63 us

profile of v1, /device:TPU:0, one launch (start us, length us, event | category | flops | bytes accessed | tf_op | source)
XLA Modules:
  0.0 57.4 jit_solution(2858257757097670420)
XLA Ops:
  0.6 52.1 %shard_map.41 = (f32[512,1024]{1,0:T(8,128)}, f32[512,1024]{1,0:T(8,128)}) custom-call(f32[128,256]{1,0:T(8,128)} %emb.1, s32[4,128]{1,0:T(4,128)} %bitcast.1), custom_call_target="tpu_custom_call" | custom-call | flops 805306368 | bytes 4194304 | tf_op jit(solution)/shard_map/pallas_call | solution.py:345
  52.8 0.0 copy-start
  52.8 3.3 %copy.6 = f32[512,1024]{1,0:T(8,128)} copy(f32[512,1024]{1,0:T(8,128)} %get-tuple-element.4) | data formatting | bytes 4194304
  56.1 0.0 copy-done
  56.1 1.3 %copy.7 = f32[512,1024]{1,0:T(8,128)} copy(f32[512,1024]{1,0:T(8,128)S(1)} %copy-done) | data formatting | bytes 4194304
Async XLA Ops:
  52.8 3.3 %copy-start = (f32[512,1024]{1,0:T(8,128)S(1)}, f32[512,1024]{1,0:T(8,128)}, u32[]{:S(2)}) copy-start(f32[512,1024]{1,0:T(8,128)} %get-tuple-element.5) | copy-start | bytes 6291460

commit v2 on v1

--- a/solution.py
+++ b/solution.py
@@ -15,9 +15,9 @@
 
 
 def kernel(
-    n_row, n_col, emb, levels, resp_out, avail_out,
-    cols, zbuf, rows, cols_cat, rows_cat, sim, resp, avail, best, second, tops, sums,
-    zs, zr, cs, cr, fs, rs, rr, ts, tr, us, ur, outs, local,
+    n_row, n_col, emb, levels, resp, avail, final,
+    cols, zbuf, rows, cols_cat, rows_cat, sim, best, second, tops, sums,
+    zs, zr, zd, cs, cr, fs, rs, rr, ts, tr, us, ur, local,
 ):
     span, width = emb.shape
     row_count, col_count = sim.shape
@@ -51,47 +51,74 @@
             send_sem=send, recv_sem=cr.at[block], device_id=(target, c), device_id_type=MESH,
         )
 
-    def z_copy(o, slot):
+    def z_copy(source, send, slot, target):
         return pltpu.make_async_remote_copy(
-            src_ref=cols.at[part(r), :], dst_ref=zbuf.at[slot],
-            send_sem=zs.at[o], recv_sem=zr.at[slot], device_id=(r, at_col(o)), device_id_type=MESH,
-        )
-
-    def row_copy(o, slot, place, target):
+            src_ref=source, dst_ref=zbuf.at[slot],
+            send_sem=send, recv_sem=zr.at[slot], device_id=(r, target), device_id_type=MESH,
+        )
+
+    def row_copy(slot, place, target):
         return pltpu.make_async_remote_copy(
             src_ref=zbuf.at[slot], dst_ref=rows.at[part(place), :],
-            send_sem=rs.at[o], recv_sem=rr.at[place], device_id=(target, c), device_id_type=MESH,
+            send_sem=rs.at[slot], recv_sem=rr.at[place], device_id=(target, c), device_id_type=MESH,
         )
 
     half = n_row // 2
-    for o in range(1, n_col):
-        z_copy(o, c).start()
+    mine = cols.at[part(r), :]
+    place = lax.rem(r, n_col)
+
+    def z_own(way):
+        return z_copy(mine, zd.at[(way + 1) // 2], c, c + way)
+
+    def z_pass(slot, way):
+        return z_copy(zbuf.at[slot], zs.at[slot], slot, c + way)
+
+    def inside(index):
+        return (index >= 0) & (index < n_col)
+
+    for way in (1, -1):
+
+        @pl.when(inside(c + way))
+        def _():
+            z_own(way).start()
+
     for o in range(1, half):
         col_copy(r, cs.at[o], at_row(2 * o)).start()
     col_copy(r, cs.at[0], sibling).start()
 
-    place = lax.rem(r, n_col)
-
-    def target_of(o):
-        slot = at_col(n_col - o)
-        return slot, slot * per + r // n_col
-
-    for o in range(1, half):
+    def col_step(o):
         source = at_row(n_row - 2 * o)
         col_copy(source, fs.at[o], sibling).wait_recv()
         col_copy(source, fs.at[o], sibling).start()
+
     for o in range(1, n_col):
-        slot, target = target_of(o)
-        z_copy(o, slot).wait_recv()
-
-        @pl.when(target != r)
-        def _():
-            row_copy(o, slot, place, target).start()
-
-        @pl.when(target == r)
-        def _():
-            pltpu.make_async_copy(zbuf.at[slot], rows.at[part(place), :], local).start()
-            pltpu.make_async_copy(zbuf.at[slot], rows.at[part(place), :], local).wait()
+        for way in (1, -1):
+            slot = c - way * o
+
+            @pl.when(inside(slot))
+            def _():
+                z_copy(mine, zs.at[slot], slot, c).wait_recv()
+
+                @pl.when(inside(c + way))
+                def _():
+                    z_pass(slot, way).start()
+
+                target = slot * per + r // n_col
+
+                @pl.when(target != r)
+                def _():
+                    row_copy(slot, place, target).start()
+
+                @pl.when(target == r)
+                def _():
+                    move = pltpu.make_async_copy(zbuf.at[slot], rows.at[part(place), :], local)
+                    move.start()
+                    move.wait()
+
+        if o < half:
+            col_step(o)
+    for o in range(n_col, half):
+        col_step(o)
 
     col_copy(sibling, cs.at[0], sibling).wait_recv()
     for o in range(1, half):
@@ -121,7 +148,7 @@
 
             @pl.when(first + q != r)
             def _():
-                row_copy(0, c, q, sibling).wait_recv()
+                row_copy(c, q, sibling).wait_recv()
 
     high, low = split(rows)
     rows_cat[:, :width] = high
@@ -285,40 +312,30 @@
     top_pass(second_entry)
     tops_sent.append(top_exchange(1))
     resp_pass(1)
-    resp_copy = pltpu.make_async_copy(resp, resp_out, local)
-    for o in range(1, n_row):
-        sum_copy(1, o, r).start()
-    resp_copy.start()
-    for o in range(1, n_row):
-        sum_copy(1, o, at_row(n_row - o)).wait_recv()
-    total = sums[1, 0]
-    for q in range(1, n_row):
-        total = total + sums[1, q]
-    positive = total[:chunks, :]
-    last = (positive, total[chunks:, :] + positive)
-
-    def out_copy(g):
-        piece = pl.ds(g * LANES, LANES)
-        return pltpu.make_async_copy(avail.at[piece, :], avail_out.at[piece, :], outs.at[g])
-
-    for g in range(groups):
-
-        @pl.loop(g * (LANES // STEP), (g + 1) * (LANES // STEP))
-        def _(i):
-            here = rows_at(i)
-            for k in range(chunks):
-                lanes = lanes_of(k)
-                avail[here, lanes] = 0.5 * avail[here, lanes] + 0.5 * renewed(last, i, here, k)
-
-        out_copy(g).start()
-
-    for o in range(1, n_col):
-        z_copy(o, c).wait_send()
-        slot, target = target_of(o)
-
-        @pl.when(target != r)
+    positive, both = sum_exchange(1)
+    final[:chunks, :] = positive
+    final[chunks:, :] = both
+
+    for way in (1, -1):
+
+        @pl.when(inside(c + way))
         def _():
-            row_copy(o, slot, place, target).wait_send()
+            z_own(way).wait_send()
+
+        for o in range(1, n_col):
+            slot = c - way * o
+
+            @pl.when(inside(slot))
+            def _():
+                @pl.when(inside(c + way))
+                def _():
+                    z_pass(slot, way).wait_send()
+
+                target = slot * per + r // n_col
+
+                @pl.when(target != r)
+                def _():
+                    row_copy(slot, place, target).wait_send()
 
     for o in range(1, half):
         col_copy(r, cs.at[o], at_row(2 * o)).wait_send()
@@ -329,9 +346,6 @@
     for turn in range(ITERS):
         for o in range(1, n_row):
             sum_copy(turn, o, r).wait_send()
-    resp_copy.wait()
-    for g in range(groups):
-        out_copy(g).wait()
 
 
 def shards(embeddings, levels):
@@ -340,13 +354,14 @@
     row_count = levels.shape[0]
     col_count = span * n_row
     groups, chunks = row_count // LANES, col_count // LANES
-    full = jax.ShapeDtypeStruct((row_count, col_count), jnp.float32)
+    full = pltpu.VMEM((row_count, col_count), jnp.float32)
     dma = pltpu.SemaphoreType.DMA
-    return pl.pallas_call(
+    scratch = 4 * row_count * col_count + 10 * (row_count + col_count) * width
+    resp, avail, final = pl.pallas_call(
         functools.partial(kernel, n_row, n_col),
-        out_shape=(full, full),
+        out_shape=(full, full, pltpu.VMEM((2 * chunks, LANES), jnp.float32)),
         in_specs=[pl.BlockSpec(memory_space=pltpu.VMEM)] * 2,
-        out_specs=[pl.BlockSpec(memory_space=pl.ANY)] * 2,
+        out_specs=[pl.BlockSpec(memory_space=pltpu.VMEM)] * 3,
         scratch_shapes=[
             pltpu.VMEM((col_count, width), jnp.float32),
             pltpu.VMEM((n_col, span, width), jnp.float32),
@@ -354,21 +369,19 @@
             pltpu.VMEM((col_count, 3 * width), jnp.bfloat16),
             pltpu.VMEM((row_count, 3 * width), jnp.bfloat16),
             pltpu.VMEM((row_count, col_count), jnp.float32),
-            pltpu.VMEM((row_count, col_count), jnp.float32),
-            pltpu.VMEM((row_count, col_count), jnp.float32),
             pltpu.VMEM((row_count, LANES), jnp.float32),
             pltpu.VMEM((row_count, LANES), jnp.float32),
             pltpu.VMEM((ITERS, n_col, 2 * groups, LANES), jnp.float32),
             pltpu.VMEM((ITERS, n_row, 2 * chunks, LANES), jnp.float32),
-            dma((n_col,)), dma((n_col,)),
+            dma((n_col,)), dma((n_col,)), dma((2,)),
             dma((n_row,)), dma((n_row,)), dma((n_row,)),
             dma((n_col,)), dma((n_col,)),
             dma((ITERS, n_col)), dma((ITERS, n_col)),
             dma((ITERS, n_row)), dma((ITERS, n_row)),
-            dma((groups,)), dma,
+            dma,
         ],
         compiler_params=pltpu.CompilerParams(
-            collective_id=0, has_side_effects=True, vmem_limit_bytes=58 * 1024 * 1024
+            collective_id=0, has_side_effects=True, vmem_limit_bytes=scratch + 12 * 1024 * 1024
         ),
         cost_estimate=pl.CostEstimate(
             flops=6 * row_count * col_count * width,
@@ -376,6 +389,16 @@
             transcendentals=0,
         ),
     )(embeddings, levels.reshape(groups, LANES))
+    row = lax.axis_index("row") * row_count + jnp.arange(row_count, dtype=jnp.int32)
+    col = lax.axis_index("col") * col_count + jnp.arange(col_count, dtype=jnp.int32)
+    positive = final[:chunks].reshape(1, col_count)
+    both = final[chunks:].reshape(1, col_count)
+    renewed = jnp.where(
+        row[:, None] == col[None, :],
+        positive,
+        jnp.minimum(0.0, both - jnp.maximum(resp, 0.0)),
+    )
+    return resp, 0.5 * avail + 0.5 * renewed
 
 
 def solution(mesh):

time: 57.6 us -> 53.9 us (0.936)
  Pallas kernels: 52.1 us -> 48.3 us
  other arithmetic: 0 us -> 1.86 us
  local copies, waits for them, and re-layouts: 4.63 us -> 2.9 us
    pallas_call x1, Pallas kernels: 52.1 us -> 48.3 us  [shards(): pl.pallas_call(functools.partial(kernel, n_row, n_col), out_shape=(full,...]
    add x0 -> x3, other arithmetic: none -> 1.86 us  [the longest x1 1.84 us: shards(): return (resp, 0.5 * avail + 0.5 * renewed)]
    unnamed x4 -> x5, local copies, waits for them, and re-layouts: 4.63 us -> 2.9 us
where the time goes in v2:
time: 53.9 us; the launch traced here: 53.7 us
  Pallas kernels  48.3 us (90%)
  local copies, waits for them, and re-layouts  2.9 us (5%)
  other arithmetic  1.86 us (3%)
  between operations  0.68 us (1%)
    pallas_call x1, Pallas kernels, shards(): pl.pallas_call(functools.partial(kernel, n_row, n_col), out_shape=(full,...  48.3 us
    unnamed x5, local copies, waits for them, and re-layouts  2.9 us
    add x1, other arithmetic, shards(): return (resp, 0.5 * avail + 0.5 * renewed)  1.84 us

profile of v2, /device:TPU:0, one launch (start us, length us, event | category | flops | bytes accessed | tf_op | source)
XLA Modules:
  0.0 53.7 jit_solution(11161244653756882016)
XLA Ops:
  0.7 0.0 copy-start
  0.7 0.9 %copy-done = f32[128,256]{1,0:T(8,128)S(1)} copy-done((f32[128,256]{1,0:T(8,128)S(1)}, f32[128,256]{1,0:T(8,128)}, u32[]{:S(2)}) %copy-start) | copy-done | bytes 131096
  1.6 0.0 copy-start.1
  1.6 0.7 %copy-done.1 = s32[512]{0:T(512)S(1)} copy-done((s32[512]{0:T(512)S(1)}, s32[512]{0:T(512)}, u32[]{:S(2)}) %copy-start.1) | copy-done | bytes 2072
  2.2 48.3 %shard_map.41 = (f32[512,1024]{1,0:T(8,128)S(1)}, f32[512,1024]{1,0:T(8,128)S(1)}, f32[16,128]{1,0:T(8,128)S(1)}) custom-call(f32[128,256]{1,0:T(8,128)S(1)} %copy-done, s32[4,128]{1,0:T(4,128)S(1)} %bitcast.5), custom_call_target="tpu_custom_call" | custom-call | flops 805306368 | bytes 4194304 | tf_op jit(solution)/shard_map/pallas_call | solution.py:360
  50.5 1.8 %add_multiply_fusion = f32[512,1024]{1,0:T(8,128)} fusion(f32[512,1024]{1,0:T(8,128)S(1)} %get-tuple-element.6, f32[512,1024]{1,0:T(8,128)S(1)} %get-tuple-element.10, f32[1024]{0:T(1024)S(1)} %get-tuple-element.9, f32[1024]{0:T(1024)S(1)} %get-tuple-element.8, s32[1024]{0:T(1024)S(1)} %iota_add_fusion, s32[512]{0:T(512)S(1)} %iota_add_fusion.1), kind=kLoop, calls=%fused_computation | loop fusion | flops 3670016 | bytes 6305792 | tf_op jit(solution)/shard_map/add | solution.py:401
  52.4 1.3 %copy.5 = f32[512,1024]{1,0:T(8,128)} copy(f32[512,1024]{1,0:T(8,128)S(1)} %get-tuple-element.10) | data formatting | bytes 4194304
  (3 shorter events, 0.0 us)
Async XLA Ops:
  0.7 0.9 %copy-start = (f32[128,256]{1,0:T(8,128)S(1)}, f32[128,256]{1,0:T(8,128)}, u32[]{:S(2)}) copy-start(f32[128,256]{1,0:T(8,128)} %emb.1) | copy-start | bytes 393220
  1.6 0.7 %copy-start.1 = (s32[512]{0:T(512)S(1)}, s32[512]{0:T(512)}, u32[]{:S(2)}) copy-start(s32[512]{0:T(512)} %param.3) | copy-start | bytes 6148

commit v3 on v2

--- a/solution.py
+++ b/solution.py
@@ -10,14 +10,15 @@
 ITERS = 2
 LANES = 128
 STEP = 32
+PIECES = 2
 LOWEST = -1e30
 MESH = pl.DeviceIdType.MESH
 
 
 def kernel(
-    n_row, n_col, emb, levels, resp, avail, final,
-    cols, zbuf, rows, cols_cat, rows_cat, sim, best, second, tops, sums,
-    zs, zr, zd, cs, cr, fs, rs, rr, ts, tr, us, ur, local,
+    n_row, n_col, emb_hbm, levels_hbm, resp, avail, final,
+    emb, levels, cols, zbuf, rows, cols_cat, rows_cat, sim, best, second, tops, sums,
+    zs, zr, zd, cs, cr, fs, rs, rr, ts, tr, us, ur, local, entry,
 ):
     span, width = emb.shape
     row_count, col_count = sim.shape
@@ -32,6 +33,10 @@
     def at_col(o):
         return lax.rem(c + o, n_col)
 
+    emb_copy = pltpu.make_async_copy(emb_hbm, emb, entry.at[0])
+    levels_copy = pltpu.make_async_copy(levels_hbm, levels, entry.at[1])
+    emb_copy.start()
+    levels_copy.start()
     barrier = pltpu.get_barrier_semaphore()
     for o in range(1, n_row):
         pl.semaphore_signal(barrier, inc=1, device_id=(at_row(o), c), device_id_type=MESH)
@@ -41,8 +46,10 @@
     def part(index):
         return pl.ds(pl.multiple_of(index * span, span), span)
 
+    emb_copy.wait()
     own = emb[...]
     cols[part(r), :] = own * lax.rsqrt(jnp.sum(own * own, axis=1, keepdims=True) + 1e-06)
+    levels_copy.wait()
     pl.semaphore_wait(barrier, n_row + n_col - 2)
 
     def col_copy(block, send, target):
@@ -51,27 +58,32 @@
             send_sem=send, recv_sem=cr.at[block], device_id=(target, c), device_id_type=MESH,
         )
 
-    def z_copy(source, send, slot, target):
+    piece = span // PIECES
+
+    def z_copy(source, send, slot, h, target):
         return pltpu.make_async_remote_copy(
-            src_ref=source, dst_ref=zbuf.at[slot],
-            send_sem=send, recv_sem=zr.at[slot], device_id=(r, target), device_id_type=MESH,
-        )
-
-    def row_copy(slot, place, target):
+            src_ref=source, dst_ref=zbuf.at[slot, pl.ds(h * piece, piece)],
+            send_sem=send, recv_sem=zr.at[slot, h], device_id=(r, target), device_id_type=MESH,
+        )
+
+    def row_part(place, h):
+        return pl.ds(pl.multiple_of(place * span + h * piece, piece), piece)
+
+    def row_copy(slot, place, h, target):
         return pltpu.make_async_remote_copy(
-            src_ref=zbuf.at[slot], dst_ref=rows.at[part(place), :],
-            send_sem=rs.at[slot], recv_sem=rr.at[place], device_id=(target, c), device_id_type=MESH,
+            src_ref=zbuf.at[slot, pl.ds(h * piece, piece)], dst_ref=rows.at[row_part(place, h), :],
+            send_sem=rs.at[slot, h], recv_sem=rr.at[place, h],
+            device_id=(target, c), device_id_type=MESH,
         )
 
     half = n_row // 2
-    mine = cols.at[part(r), :]
     place = lax.rem(r, n_col)
 
-    def z_own(way):
-        return z_copy(mine, zd.at[(way + 1) // 2], c, c + way)
-
-    def z_pass(slot, way):
-        return z_copy(zbuf.at[slot], zs.at[slot], slot, c + way)
+    def z_own(way, h):
+        return z_copy(cols.at[row_part(r, h), :], zd.at[(way + 1) // 2, h], c, h, c + way)
+
+    def z_pass(slot, way, h):
+        return z_copy(zbuf.at[slot, pl.ds(h * piece, piece)], zs.at[slot, h], slot, h, c + way)
 
     def inside(index):
         return (index >= 0) & (index < n_col)
@@ -80,7 +92,8 @@
 
         @pl.when(inside(c + way))
         def _():
-            z_own(way).start()
+            for h in range(PIECES):
+                z_own(way, h).start()
 
     for o in range(1, half):
         col_copy(r, cs.at[o], at_row(2 * o)).start()
@@ -92,28 +105,33 @@
         col_copy(source, fs.at[o], sibling).start()
 
     for o in range(1, n_col):
-        for way in (1, -1):
-            slot = c - way * o
-
-            @pl.when(inside(slot))
-            def _():
-                z_copy(mine, zs.at[slot], slot, c).wait_recv()
-
-                @pl.when(inside(c + way))
+        for h in range(PIECES):
+            for way in (1, -1):
+                slot = c - way * o
+
+                @pl.when(inside(slot))
                 def _():
-                    z_pass(slot, way).start()
-
-                target = slot * per + r // n_col
-
-                @pl.when(target != r)
-                def _():
-                    row_copy(slot, place, target).start()
-
-                @pl.when(target == r)
-                def _():
-                    move = pltpu.make_async_copy(zbuf.at[slot], rows.at[part(place), :], local)
-                    move.start()
-                    move.wait()
+                    z_copy(cols.at[row_part(r, h), :], zs.at[slot, h], slot, h, c).wait_recv()
+
+                    @pl.when(inside(c + way))
+                    def _():
+                        z_pass(slot, way, h).start()
+
+                    target = slot * per + r // n_col
+
+                    @pl.when(target != r)
+                    def _():
+                        row_copy(slot, place, h, target).start()
+
+                    @pl.when(target == r)
+                    def _():
+                        move = pltpu.make_async_copy(
+                            zbuf.at[slot, pl.ds(h * piece, piece)],
+                            rows.at[row_part(place, h), :],
+                            local,
+                        )
+                        move.start()
+                        move.wait()
 
         if o < half:
             col_step(o)
@@ -148,7 +166,8 @@
 
             @pl.when(first + q != r)
             def _():
-                row_copy(c, q, sibling).wait_recv()
+                for h in range(PIECES):
+                    row_copy(c, q, h, sibling).wait_recv()
 
     high, low = split(rows)
     rows_cat[:, :width] = high
@@ -186,9 +205,6 @@
         for g in range(groups):
             tile = tile_of(g)
             sim[tile] = jnp.where(eye, preference[g : g + 1, :], sim[tile])
-
-    def spread(value):
-        return jnp.broadcast_to(value, (value.shape[0], LANES))
 
     def lanes_of(k):
         return pl.ds(k * LANES, LANES)
@@ -206,20 +222,20 @@
                 value = entry(i, here, k)
                 two = jnp.maximum(two, jnp.minimum(one, value))
                 one = jnp.maximum(one, value)
-            top = jnp.max(one, axis=1, keepdims=True)
-            count = jnp.sum(jnp.where(one == top, 1.0, 0.0), axis=1, keepdims=True)
-            rest = jnp.max(
-                jnp.maximum(jnp.where(one < top, one, LOWEST), two), axis=1, keepdims=True
-            )
-            best[here, :] = spread(top)
-            second[here, :] = spread(jnp.where(count > 1.0, top, rest))
+            best[here, :] = one
+            second[here, :] = two
 
     def top_exchange(turn):
         for g in range(groups):
-            for ref, base in ((best, 0), (second, groups)):
-                tops[turn, c, base + g : base + g + 1, :] = jnp.sum(
-                    jnp.where(eye, ref[g * LANES : (g + 1) * LANES, :], 0.0), axis=0, keepdims=True
-                )
+            tile = slice(g * LANES, (g + 1) * LANES)
+            one, two = best[tile, :].T, second[tile, :].T
+            top = jnp.max(one, axis=0, keepdims=True)
+            count = jnp.sum(jnp.where(one == top, 1.0, 0.0), axis=0, keepdims=True)
+            rest = jnp.max(
+                jnp.maximum(jnp.where(one < top, one, LOWEST), two), axis=0, keepdims=True
+            )
+            tops[turn, c, g : g + 1, :] = top
+            tops[turn, c, groups + g : groups + g + 1, :] = jnp.where(count > 1.0, top, rest)
 
         def copy(o, slot):
             return pltpu.make_async_remote_copy(
@@ -239,9 +255,9 @@
             one = jnp.maximum(one, other)
         for g in range(groups):
             for ref, value in ((best, one), (second, two)):
-                ref[g * LANES : (g + 1) * LANES, :] = spread(
-                    jnp.sum(jnp.where(eye, value[g : g + 1, :], 0.0), axis=1, keepdims=True)
-                )
+                ref[g * LANES : (g + 1) * LANES, :] = jnp.broadcast_to(
+                    value[g : g + 1, :], (LANES, LANES)
+                ).T
         return lambda: [copy(o, c).wait_send() for o in range(1, n_col)]
 
     def resp_pass(turn):
@@ -320,7 +336,8 @@
 
         @pl.when(inside(c + way))
         def _():
-            z_own(way).wait_send()
+            for h in range(PIECES):
+                z_own(way, h).wait_send()
 
         for o in range(1, n_col):
             slot = c - way * o
@@ -329,13 +346,15 @@
             def _():
                 @pl.when(inside(c + way))
                 def _():
-                    z_pass(slot, way).wait_send()
+                    for h in range(PIECES):
+                        z_pass(slot, way, h).wait_send()
 
                 target = slot * per + r // n_col
 
                 @pl.when(target != r)
                 def _():
-                    row_copy(slot, place, target).wait_send()
+                    for h in range(PIECES):
+                        row_copy(slot, place, h, target).wait_send()
 
     for o in range(1, half):
         col_copy(r, cs.at[o], at_row(2 * o)).wait_send()
@@ -360,9 +379,11 @@
     resp, avail, final = pl.pallas_call(
         functools.partial(kernel, n_row, n_col),
         out_shape=(full, full, pltpu.VMEM((2 * chunks, LANES), jnp.float32)),
-        in_specs=[pl.BlockSpec(memory_space=pltpu.VMEM)] * 2,
+        in_specs=[pl.BlockSpec(memory_space=pltpu.HBM)] * 2,
         out_specs=[pl.BlockSpec(memory_space=pltpu.VMEM)] * 3,
         scratch_shapes=[
+            pltpu.VMEM((span, width), jnp.float32),
+            pltpu.VMEM((groups, LANES), jnp.int32),
             pltpu.VMEM((col_count, width), jnp.float32),
             pltpu.VMEM((n_col, span, width), jnp.float32),
             pltpu.VMEM((row_count, width), jnp.float32),
@@ -373,12 +394,12 @@
             pltpu.VMEM((row_count, LANES), jnp.float32),
             pltpu.VMEM((ITERS, n_col, 2 * groups, LANES), jnp.float32),
             pltpu.VMEM((ITERS, n_row, 2 * chunks, LANES), jnp.float32),
-            dma((n_col,)), dma((n_col,)), dma((2,)),
+            dma((n_col, PIECES)), dma((n_col, PIECES)), dma((2, PIECES)),
             dma((n_row,)), dma((n_row,)), dma((n_row,)),
-            dma((n_col,)), dma((n_col,)),
+            dma((n_col, PIECES)), dma((n_col, PIECES)),
             dma((ITERS, n_col)), dma((ITERS, n_col)),
             dma((ITERS, n_row)), dma((ITERS, n_row)),
-            dma,
+            dma, dma((2,)),
         ],
         compiler_params=pltpu.CompilerParams(
             collective_id=0, has_side_effects=True, vmem_limit_bytes=scratch + 12 * 1024 * 1024

time: 53.9 us -> 48.3 us (0.90)
  Pallas kernels: 48.3 us -> 42.7 us
    pallas_call x1, Pallas kernels: 48.3 us -> 42.7 us  [shards(): pl.pallas_call(functools.partial(kernel, n_row, n_col), out_shape=(full,...]
where the time goes in v3:
time: 48.3 us; the launch traced here: 48.1 us
  Pallas kernels  42.7 us (88%)
  local copies, waits for them, and re-layouts  2.9 us (6%)
  other arithmetic  1.86 us (4%)
  between operations  0.68 us (1%)
    pallas_call x1, Pallas kernels, shards(): pl.pallas_call(functools.partial(kernel, n_row, n_col), out_shape=(full,...  42.7 us
    unnamed x5, local copies, waits for them, and re-layouts  2.9 us
    add x1, other arithmetic, shards(): return (resp, 0.5 * avail + 0.5 * renewed)  1.84 us

profile of v3, /device:TPU:0, one launch (start us, length us, event | category | flops | bytes accessed | tf_op | source)
XLA Modules:
  0.0 48.1 jit_solution(14250040767673919842)
XLA Ops:
  0.7 0.0 copy-start
  0.7 0.9 %copy-done = f32[128,256]{1,0:T(8,128)S(1)} copy-done((f32[128,256]{1,0:T(8,128)S(1)}, f32[128,256]{1,0:T(8,128)}, u32[]{:S(2)}) %copy-start) | copy-done | bytes 131096
  1.6 0.0 copy-start.1
  1.6 0.7 %copy-done.1 = s32[512]{0:T(512)S(1)} copy-done((s32[512]{0:T(512)S(1)}, s32[512]{0:T(512)}, u32[]{:S(2)}) %copy-start.1) | copy-done | bytes 2072
  2.2 42.7 %shard_map.41 = (f32[512,1024]{1,0:T(8,128)S(1)}, f32[512,1024]{1,0:T(8,128)S(1)}, f32[16,128]{1,0:T(8,128)S(1)}) custom-call(f32[128,256]{1,0:T(8,128)S(1)} %copy-done, s32[4,128]{1,0:T(4,128)S(1)} %bitcast.5), custom_call_target="tpu_custom_call" | custom-call | flops 805306368 | bytes 4194304 | tf_op jit(solution)/shard_map/pallas_call | solution.py:379
  44.9 1.8 %add_multiply_fusion = f32[512,1024]{1,0:T(8,128)} fusion(f32[512,1024]{1,0:T(8,128)S(1)} %get-tuple-element.6, f32[512,1024]{1,0:T(8,128)S(1)} %get-tuple-element.10, f32[1024]{0:T(1024)S(1)} %get-tuple-element.9, f32[1024]{0:T(1024)S(1)} %get-tuple-element.8, s32[1024]{0:T(1024)S(1)} %iota_add_fusion, s32[512]{0:T(512)S(1)} %iota_add_fusion.1), kind=kLoop, calls=%fused_computation | loop fusion | flops 3670016 | bytes 6305792 | tf_op jit(solution)/shard_map/add | solution.py:422
  46.8 1.3 %copy.5 = f32[512,1024]{1,0:T(8,128)} copy(f32[512,1024]{1,0:T(8,128)S(1)} %get-tuple-element.10) | data formatting | bytes 4194304
  (3 shorter events, 0.0 us)
Async XLA Ops:
  0.7 0.9 %copy-start = (f32[128,256]{1,0:T(8,128)S(1)}, f32[128,256]{1,0:T(8,128)}, u32[]{:S(2)}) copy-start(f32[128,256]{1,0:T(8,128)} %emb_hbm.1) | copy-start | bytes 393220
  1.6 0.7 %copy-start.1 = (s32[512]{0:T(512)S(1)}, s32[512]{0:T(512)}, u32[]{:S(2)}) copy-start(s32[512]{0:T(512)} %param.3) | copy-start | bytes 6148

commit v4 on v3

--- a/solution.py
+++ b/solution.py
@@ -10,7 +10,7 @@
 ITERS = 2
 LANES = 128
 STEP = 32
-PIECES = 2
+PIECES = 4
 LOWEST = -1e30
 MESH = pl.DeviceIdType.MESH
 
@@ -375,7 +375,6 @@
     groups, chunks = row_count // LANES, col_count // LANES
     full = pltpu.VMEM((row_count, col_count), jnp.float32)
     dma = pltpu.SemaphoreType.DMA
-    scratch = 4 * row_count * col_count + 10 * (row_count + col_count) * width
     resp, avail, final = pl.pallas_call(
         functools.partial(kernel, n_row, n_col),
         out_shape=(full, full, pltpu.VMEM((2 * chunks, LANES), jnp.float32)),
@@ -402,7 +401,7 @@
             dma, dma((2,)),
         ],
         compiler_params=pltpu.CompilerParams(
-            collective_id=0, has_side_effects=True, vmem_limit_bytes=scratch + 12 * 1024 * 1024
+            collective_id=0, has_side_effects=True, vmem_limit_bytes=58 * 1024 * 1024 - 8 * row_count * col_count
         ),
         cost_estimate=pl.CostEstimate(
             flops=6 * row_count * col_count * width,

time: 48.3 us -> 45.6 us (0.944)
  local copies, waits for them, and re-layouts: 2.9 us -> 1.32 us
  Pallas kernels: 42.7 us -> 41.6 us
    unnamed x5 -> x1, local copies, waits for them, and re-layouts: 2.9 us -> 1.32 us
    pallas_call x1, Pallas kernels: 42.7 us -> 41.6 us  [shards(): pl.pallas_call(functools.partial(kernel, n_row, n_col), out_shape=(full,...]
where the time goes in v4:
time: 45.6 us; the launch traced here: 45.5 us
  Pallas kernels  41.6 us (91%)
  other arithmetic  1.87 us (4%)
  local copies, waits for them, and re-layouts  1.32 us (3%)
  between operations  0.67 us (1%)
    pallas_call x1, Pallas kernels, shards(): pl.pallas_call(functools.partial(kernel, n_row, n_col), out_shape=(full,...  41.6 us
    add x1, other arithmetic, shards(): return (resp, 0.5 * avail + 0.5 * renewed)  1.86 us
    unnamed x1, local copies, waits for them, and re-layouts  1.32 us

profile of v4, /device:TPU:0, one launch (start us, length us, event | category | flops | bytes accessed | tf_op | source)
XLA Modules:
  0.0 45.5 jit_solution(9035067262061277731)
XLA Ops:
  0.7 41.6 %shard_map.41 = (f32[512,1024]{1,0:T(8,128)S(1)}, f32[512,1024]{1,0:T(8,128)S(1)}, f32[16,128]{1,0:T(8,128)S(1)}) custom-call(f32[128,256]{1,0:T(8,128)} %emb_hbm.1, s32[4,128]{1,0:T(4,128)} %bitcast.5), custom_call_target="tpu_custom_call" | custom-call | flops 805306368 | bytes 4194304 | tf_op jit(solution)/shard_map/pallas_call | solution.py:378
  42.3 1.9 %add_multiply_fusion = f32[512,1024]{1,0:T(8,128)} fusion(f32[512,1024]{1,0:T(8,128)S(1)} %get-tuple-element.6, f32[512,1024]{1,0:T(8,128)S(1)} %get-tuple-element.10, f32[1024]{0:T(1024)S(1)} %get-tuple-element.9, f32[1024]{0:T(1024)S(1)} %get-tuple-element.8, s32[1024]{0:T(1024)S(1)} %iota_add_fusion, s32[512]{0:T(512)S(1)} %iota_add_fusion.1), kind=kLoop, calls=%fused_computation | loop fusion | flops 3670016 | bytes 6305792 | tf_op jit(solution)/shard_map/add | solution.py:421
  44.2 1.3 %copy.5 = f32[512,1024]{1,0:T(8,128)} copy(f32[512,1024]{1,0:T(8,128)S(1)} %get-tuple-element.10) | data formatting | bytes 4194304
  (3 shorter events, 0.0 us)

commit v5 on v4

--- a/solution.py
+++ b/solution.py
@@ -277,7 +277,7 @@
                 return total + jnp.sum(positive.reshape(STEP // 8, 8, LANES), axis=0)
 
             total = lax.fori_loop(
-                0, row_count // STEP, body, jnp.zeros((8, LANES), jnp.float32), unroll=2
+                0, row_count // STEP, body, jnp.zeros((8, LANES), jnp.float32), unroll=8
             )
             sums[turn, r, k : k + 1, :] = jnp.sum(total, axis=0, keepdims=True)
         sums[turn, r, chunks:, :] = jnp.zeros((chunks, LANES), jnp.float32)
@@ -365,6 +365,43 @@
     for turn in range(ITERS):
         for o in range(1, n_row):
             sum_copy(turn, o, r).wait_send()
+
+
+def finish(offset_ref, resp, avail, final, resp_out, avail_out, held, sems):
+    row_count, col_count = resp.shape
+    groups, chunks = row_count // LANES, col_count // LANES
+    offset = offset_ref[0]
+    resp_copy = pltpu.make_async_copy(resp, resp_out, sems.at[groups])
+    resp_copy.start()
+    slant = lax.broadcasted_iota(jnp.int32, (STEP, LANES), 1) - lax.broadcasted_iota(
+        jnp.int32, (STEP, LANES), 0
+    )
+    copies = []
+    for g in range(groups):
+
+        @pl.loop(g * (LANES // STEP), (g + 1) * (LANES // STEP))
+        def _(i):
+            here = pl.ds(pl.multiple_of(i * STEP, STEP), STEP)
+            for k in range(chunks):
+                lanes = pl.ds(k * LANES, LANES)
+                renewed = jnp.where(
+                    slant == offset + i * STEP - k * LANES,
+                    final[k : k + 1, :],
+                    jnp.minimum(
+                        0.0,
+                        final[chunks + k : chunks + k + 1, :] - jnp.maximum(resp[here, lanes], 0.0),
+                    ),
+                )
+                held[here, lanes] = 0.5 * avail[here, lanes] + 0.5 * renewed
+
+        piece = pl.ds(g * LANES, LANES)
+        copies.append(
+            pltpu.make_async_copy(held.at[piece, :], avail_out.at[piece, :], sems.at[g])
+        )
+        copies[-1].start()
+    resp_copy.wait()
+    for copy in copies:
+        copy.wait()
 
 
 def shards(embeddings, levels):
@@ -409,16 +446,19 @@
             transcendentals=0,
         ),
     )(embeddings, levels.reshape(groups, LANES))
-    row = lax.axis_index("row") * row_count + jnp.arange(row_count, dtype=jnp.int32)
-    col = lax.axis_index("col") * col_count + jnp.arange(col_count, dtype=jnp.int32)
-    positive = final[:chunks].reshape(1, col_count)
-    both = final[chunks:].reshape(1, col_count)
-    renewed = jnp.where(
-        row[:, None] == col[None, :],
-        positive,
-        jnp.minimum(0.0, both - jnp.maximum(resp, 0.0)),
-    )
-    return resp, 0.5 * avail + 0.5 * renewed
+    offset = lax.axis_index("row") * row_count - lax.axis_index("col") * col_count
+    result = jax.ShapeDtypeStruct((row_count, col_count), jnp.float32)
+    return pl.pallas_call(
+        finish,
+        out_shape=(result, result),
+        in_specs=[pl.BlockSpec(memory_space=pltpu.SMEM)]
+        + [pl.BlockSpec(memory_space=pltpu.VMEM)] * 3,
+        out_specs=[pl.BlockSpec(memory_space=pl.ANY)] * 2,
+        scratch_shapes=[pltpu.VMEM((row_count, col_count), jnp.float32), dma((groups + 1,))],
+        compiler_params=pltpu.CompilerParams(
+            vmem_limit_bytes=4 * row_count * col_count + 4 * 1024 * 1024
+        ),
+    )(offset.reshape(1), resp, avail, final)
 
 
 def solution(mesh):

time: 45.6 us -> 43.9 us (0.963)
  other arithmetic: 1.87 us -> 0 us
  Pallas kernels: 41.6 us -> 43.1 us
  local copies, waits for them, and re-layouts: 1.32 us -> 0 us
    pallas_call x0 -> x1, Pallas kernels: none -> 2.05 us  [shards(): pl.pallas_call(finish, out_shape=(result, result), in_specs=[pl.BlockSpec...]
    add x3 -> x0, other arithmetic: 1.87 us -> none  [the longest x1 1.86 us: shards(): return (resp, 0.5 * avail + 0.5 * renewed)]
    unnamed x1 -> x0, local copies, waits for them, and re-layouts: 1.32 us -> none
    pallas_call x1, Pallas kernels: 41.6 us -> 41.1 us  [shards(): pl.pallas_call(functools.partial(kernel, n_row, n_col), out_shape=(full,...]
where the time goes in v5:
time: 43.9 us; the launch traced here: 43.8 us
  Pallas kernels  43.1 us (98%)
  between operations  0.64 us (1%)
    pallas_call x1, Pallas kernels, shards(): pl.pallas_call(functools.partial(kernel, n_row, n_col), out_shape=(full,...  41.1 us
    pallas_call x1, Pallas kernels, shards(): pl.pallas_call(finish, out_shape=(result, result), in_specs=[pl.BlockSpec...  2.05 us

profile of v5, /device:TPU:0, one launch (start us, length us, event | category | flops | bytes accessed | tf_op | source)
XLA Modules:
  0.0 43.8 jit_solution(17056220069492256272)
XLA Ops:
  0.6 41.1 %shard_map.41 = (f32[512,1024]{1,0:T(8,128)S(1)}, f32[512,1024]{1,0:T(8,128)S(1)}, f32[16,128]{1,0:T(8,128)S(1)}) custom-call(f32[128,256]{1,0:T(8,128)} %emb_hbm.1, s32[4,128]{1,0:T(4,128)} %bitcast.2), custom_call_target="tpu_custom_call" | custom-call | flops 805306368 | bytes 4194304 | tf_op jit(solution)/shard_map/pallas_call | solution.py:415
  41.7 2.0 %shard_map.42 = (f32[512,1024]{1,0:T(8,128)}, f32[512,1024]{1,0:T(8,128)}) custom-call(s32[1]{0:T(128)} %bitcast.offset_ref, f32[512,1024]{1,0:T(8,128)S(1)} %get-tuple-element.5.resp, f32[512,1024]{1,0:T(8,128)S(1)} %get-tuple-element.6.avail, f32[16,128]{1,0:T(8,128)S(1)} %get-tuple-element.7.final), custom_call_target="tpu_custom_call" | custom-call | tf_op jit(solution)/shard_map/pallas_call | solution.py:451
